TPU v7x, 32 devices: a whole 2x2x4 slice. The times are simulated.
32 devices in a mesh: gx: 4 (over z), gy: 4 (over y, x), gz: 2 (over core).
Axes of the slice: x: 2, y: 2, z: 4, core: 2. Of those that a mesh axis runs over, the one named last changes fastest.
Arguments:
- offsets: float32 [3, 16, 16, 4, 128], P(None, 'gx', 'gy', 'gz'), may hold values from -0.5 to 0.5
- burgers: float32 [3, 16, 16, 4, 128], P(None, 'gx', 'gy', 'gz'), may hold values from -4 to 4
- line: float32 [3, 16, 16, 4, 128], P(None, 'gx', 'gy', 'gz'), may hold values from -3 to 3
- block_fill: int32 [16, 16, 4], P('gx', 'gy', 'gz'), may hold values from 1 to 128, as said below
- near_pairs: int32 [6144], P(('gx', 'gy', 'gz')), may hold values from 0 to 447, as said below
- pair_count: int32 [32], P(('gx', 'gy', 'gz')), may hold values from 24 to 192, as said below
Outputs:
- forces: float32 [3, 16, 16, 4, 128], P(None, 'gx', 'gy', 'gz')
Inputs may be any that keep to these rules, and one draw needn't show every extreme that they name: `block_fill`: some block in every draw holds exactly 128 live segments. `near_pairs`: within each device's 192 entries the codes are distinct; each device's first four entries are 5, 7, 9 and 447, and code 0 is among its entries. `pair_count`: some device has exactly 192 live entries.
All inputs are finite; a program needn't handle non-finite values.
Results may differ from a plain program's by a relative error of at most 0.0003.
Values sent between devices are 32-bit elements; how exact they have to be, the bound alone decides.
No kernel may reach another device: no remote copies, remote signals or barrier semaphores. Data moves between devices by JAX's collectives and lax.ppermute only.
A program may use at most 64 MiB of HBM per device.

v0:
```python
import functools
import math

import jax
import jax.numpy as jnp
import numpy as np
from jax import lax
from jax.experimental import pallas as pl
from jax.experimental.pallas import tpu as pltpu
from jax.sharding import PartitionSpec as P

stencil_table = (
    (0, 0, 0),
    (1, 0, 0),
    (0, 1, 0),
    (0, 0, 1),
    (1, 1, 0),
    (-1, 1, 0),
    (1, 0, 1),
    (1, 0, -1),
    (0, 1, 1),
    (0, -1, 1),
    (1, 1, -1),
    (1, -1, 1),
    (-1, 1, 1),
    (1, 1, 1),
)
code_total = len(stencil_table)
kernel_scale = 1.0 / (8.0 * math.pi)
core_square = 0.09
lanes = 128
mark = 2048.0
parts_sent = 10
unroll = 64
short_steps = (16, 32, 48)
first_share = 96
f32 = jnp.float32
bf16 = jnp.bfloat16


group_set = (0, 1, 1, 2, 2, 1, 1, 1, 2, 2)


def set_groups(which):
    return [g for g in range(10) if group_set[g] == which]


def group_heights(bx, by, bz):
    return [bx * by * bz, by * bz, by * bz, (bx + 2) * bz, (bx + 2) * bz] * 2


def block_layout(bx, by, bz):
    coords = []
    for z_of in ([z + 1 for z in range(bz)], [bz + 1 if z == 0 else 0 for z in range(bz)]):
        coords.append([(x + 1, y + 1, z) for x in range(bx) for y in range(by) for z in z_of])
        for x in (0, bx + 1):
            coords.append([(x, y + 1, z) for y in range(by) for z in z_of])
        for y in (0, by + 1):
            coords.append([(x, y, z) for x in range(bx + 2) for z in z_of])
    return coords


def work_tables(bx, by, bz):
    groups = block_layout(bx, by, bz)
    place = {}
    count = [0, 0, 0]
    for g, group in enumerate(groups):
        for c in group:
            place[c] = (group_set[g], count[group_set[g]])
            count[group_set[g]] += 1
    codes = np.zeros((8, count[0] * code_total), np.float32)
    for a, at in enumerate(groups[0]):
        for code, o in enumerate(stencil_table):
            which, b = place[tuple(at[d] + o[d] for d in range(3))]
            k = a * code_total + code
            codes[:2, k] = a, b
            codes[(2, 4, 5)[which], k] = 1.0
            codes[3, k] = which == 0 and code > 0
    inbound = []
    for which in (1, 2):
        found = []
        for at, (at_set, h) in place.items():
            for code, o in enumerate(stencil_table):
                to, b = place.get(tuple(at[d] + o[d] for d in range(3)), (3, 0))
                if at_set == which and to == 0 and code:
                    found.append((b, h, code))
        size = -(-(len(found) + 1) // 16) * 16
        ranks = np.zeros((size, (code_total - 1) * count[which]), np.float32)
        ends = np.zeros((8, size), np.float32)
        for k, (b, h, code) in enumerate(found):
            at = (code - 1) * count[which] + h
            ranks[k + 1 : len(found), at] = ranks[size - 1, at] = 1.0
            ranks[k, at] = mark
            ends[:2, k] = b, h
        inbound += [ranks, ends]
    return [codes, *inbound]


def position(group, rows, bx, by, bz):
    row = lax.broadcasted_iota(jnp.int32, (rows, lanes), 0)
    z = row % bz
    line = row // bz
    kind = group % 5
    if kind == 0:
        x, y = line // by + 1, line % by + 1
    elif kind <= 2:
        x, y = jnp.full_like(row, 0 if kind == 1 else bx + 1), line + 1
    else:
        x, y = line, jnp.full_like(row, 0 if kind == 3 else by + 1)
    if group < 5:
        z = z + 1
    else:
        z = jnp.where(z == 0, bz + 1, 0)
    sides = (bx + 1, by + 1, bz + 1)
    return [v.astype(f32) - 0.5 * side for v, side in zip((x, y, z), sides)]


def moment_rows(b, l):
    zz = b[2] * l[2]
    return [
        b[0] * l[1],
        b[0] * l[2],
        b[1] * l[0],
        b[1] * l[2],
        b[2] * l[0],
        b[2] * l[1],
        b[0] * l[0] - zz,
        b[1] * l[1] - zz,
    ]


def cross_rows(q, b, l):
    c = [q[1] * b[2] - q[2] * b[1], q[2] * b[0] - q[0] * b[2], q[0] * b[1] - q[1] * b[0]]
    return [
        2.0 * c[0] * l[0],
        2.0 * c[1] * l[1],
        2.0 * c[2] * l[2],
        c[0] * l[1] + c[1] * l[0],
        c[0] * l[2] + c[2] * l[0],
        c[1] * l[2] + c[2] * l[1],
    ]


def turn_rows(r, m):
    return [
        2.0 * (r[1] * m[4] - r[2] * m[2]),
        2.0 * (r[2] * m[0] - r[0] * m[5]),
        2.0 * (r[0] * m[3] - r[1] * m[1]),
        r[1] * m[5] - r[0] * m[4] + r[2] * (m[6] - m[7]),
        r[0] * m[2] - r[2] * m[3] - r[1] * m[6],
        r[2] * m[1] + r[0] * m[7] - r[1] * m[0],
    ]


def pieces(value):
    first = value.astype(bf16).astype(f32)
    rest = value - first
    second = rest.astype(bf16).astype(f32)
    return first, second, rest - second


def distance_rows(q):
    near = q[0] * q[0] + q[1] * q[1] + q[2] * q[2]
    one = jnp.ones_like(near)
    left, right = [], []
    for axis in q:
        p1, p2, p3 = pieces(axis)
        left += [p1, p1, p2, p2, p1, p3]
        right += [-2.0 * v for v in (p1, p2, p1, p2, p3, p1)]
    left += [*pieces(near), one, one, one]
    right += [one, one, one, *pieces(near + core_square)]
    return left, right


def pack_kernel(sizes, axes, count, fill_h, offsets_h, burgers_h, line_h, pairs_h, *refs):
    bx, by, bz, cells = sizes
    total, face = bx * by * bz, by * bz
    tables_h, (own, face_lo, face_hi, mom, pairs), tables = refs[:5], refs[5:10], refs[10:15]
    fill, offsets, burgers, line, level, sems = refs[15:]
    table_copies = [
        pltpu.make_async_copy(u, v, sems.at[5 + k]) for k, (u, v) in enumerate(zip(tables_h, tables))
    ]
    moves = ((fill_h, fill), (pairs_h, pairs), (burgers_h, burgers), (line_h, line), (offsets_h, offsets))
    copies = [pltpu.make_async_copy(u, v, sems.at[k]) for k, (u, v) in enumerate(moves)]
    for copy in copies + table_copies:
        copy.start()
    for copy in copies:
        copy.wait()
    for x in range(bx):
        for y in range(by):
            column = jnp.broadcast_to(fill[x][:, y : y + 1], (bz, lanes))
            level[x * face + y * bz : x * face + (y + 1) * bz, :] = column
    live = lax.broadcasted_iota(jnp.int32, (total, lanes), 1) < level[...]
    b, l = [], []
    for d in range(3):
        own[d] = offsets[d]
        b.append(jnp.where(live, burgers[d], 0.0))
        l.append(jnp.where(live, line[d], 0.0))
        own[3 + d] = b[d]
        own[6 + d] = l[d]
    entries = pairs.shape[1]
    code = pairs[...]
    block_no = code // code_total
    code_no = code - block_no * code_total
    alive = lax.broadcasted_iota(jnp.int32, (1, entries), 1) < count[0]
    of_block = lax.broadcasted_iota(jnp.int32, (total, entries), 0) == block_no
    of_code = lax.broadcasted_iota(jnp.int32, (lanes, entries), 0) == code_no
    own[9] = lax.dot_general(
        jnp.where(of_block & alive, 1.0, 0.0).astype(bf16),
        jnp.where(of_code, 1.0, 0.0).astype(bf16),
        (((1,), (1,)), ((), ())),
        preferred_element_type=f32,
    )
    cx, cy, cz = bx // 2, by // 2, bz // 2
    here = lax.axis_index(axes[0])
    for axis in axes[1:]:
        here = here * lax.axis_size(axis) + lax.axis_index(axis)
    first_lane = here * (cx * cy * cz)
    wide = lax.broadcasted_iota(jnp.int32, (face, lanes), 1)
    deep = lax.broadcasted_iota(jnp.int32, (face, lanes), 0)
    local = deep // (2 * bz) * cz + deep % bz // 2
    sums = []
    for feature in moment_rows(b, l):
        column = []
        for x in range(cx):
            both = feature[2 * x * face : (2 * x + 1) * face] + feature[(2 * x + 1) * face : (2 * x + 2) * face]
            column.append(jnp.sum(both, 1, keepdims=True))
        sums.append(column)
    for chunk in range(cells // lanes):
        for f, column in enumerate(sums):
            placed = jnp.zeros((face, lanes), f32)
            for x in range(cx):
                lane_of = first_lane + x * cy * cz + local - chunk * lanes
                placed = placed + jnp.where(wide == lane_of, column[x], 0.0)
            mom[chunk * 8 + f : chunk * 8 + f + 1, :] = jnp.sum(placed, 0, keepdims=True)
    for d in range(parts_sent):
        face_lo[d * face : (d + 1) * face] = own[d, 0:face]
        face_hi[d * face : (d + 1) * face] = own[d, total - face : total]
    face_lo[parts_sent * face :] = mom[...]
    face_hi[parts_sent * face :] = mom[...]
    for copy in table_copies:
        copy.wait()


def rim_kernel(sizes, both_ways, own, mom, x_lo, x_hi, *refs):
    bx, by, bz, _ = sizes
    face = by * bz
    (face_lo, face_hi, x_all, mom_x), more = refs[-4:], refs[1:-4]
    for y, out in ((0, face_lo), (by - 1, face_hi)):
        for d in range(parts_sent):
            to, at = d * (bx + 2) * bz, y * bz
            for x in range(bx + 2):
                if x == 0 or x == bx + 1:
                    start = d * face + at
                    rows = (x_lo if x == 0 else x_hi)[start : start + bz]
                else:
                    start = (x - 1) * face + at
                    rows = own[d, start : start + bz]
                out[to + x * bz : to + (x + 1) * bz] = rows
    total = bx * by * bz
    for d in range(parts_sent):
        x_all[d * total : (d + 1) * total] = own[d]
    start = parts_sent * total
    for v in (x_lo, x_hi):
        x_all[start : start + v.shape[0]] = v[...]
        start += v.shape[0]
    head = parts_sent * face
    total = mom[...] + x_lo[head:]
    if both_ways:
        total = total + x_hi[head:]
    for v in more:
        total = total + v[...]
    mom_x[...] = total
    head = parts_sent * (bx + 2) * bz
    face_lo[head:] = total
    face_hi[head:] = total


def shape_blocks(sizes, sources, stage, right, weighed, left=None):
    bx, by, bz, _ = sizes
    heights = group_heights(bx, by, bz)
    base = 0
    for group, part in sources:
        h = heights[group]
        zero = jnp.zeros((h, lanes), f32)
        place = position(group, h, bx, by, bz)
        q = [part(d) + place[d] for d in range(3)]
        b = [part(3 + d) for d in range(3)]
        l = [part(6 + d) for d in range(3)]
        rows = moment_rows(b, l) + cross_rows(q, b, l)
        lhs, rhs = distance_rows(q)
        rows = rows + [zero] * (16 - len(rows)) + rhs + [zero] * (32 - len(rhs))
        if left is not None:
            rows = rows + lhs + [zero] * (32 - len(lhs))
        for f, value in enumerate(rows):
            stage[pl.ds(base * 80 + f, h, stride=80), :] = value
        base += h

    def shape_block(block, carry):
        at = pl.multiple_of(block * 80, 16)
        product = stage[pl.ds(at, 16), :]
        high = product.astype(bf16)
        low = (product - high.astype(f32)).astype(bf16)
        weighed[block, 0:16, 0:lanes] = high
        weighed[block, 0:16, lanes : 2 * lanes] = high
        weighed[block, 16:32, 0:lanes] = low
        weighed[block, 16:32, lanes : 2 * lanes] = jnp.zeros_like(low)
        right[block] = stage[pl.ds(at + 16, 32), :].astype(bf16)
        if left is not None:
            left[block] = stage[pl.ds(at + 48, 32), :].astype(bf16)
        return carry

    lax.fori_loop(0, base, shape_block, 0, unroll=8)


def rows_of(ref, start, height):
    return lambda d: ref[start + d * height : start + (d + 1) * height, :]


def ranked(size):
    down = lax.broadcasted_iota(jnp.int32, (size, size), 0)
    across = lax.broadcasted_iota(jnp.int32, (size, size), 1)
    return jnp.where(down > across, 1.0, jnp.where(down == across, mark, 0.0)).astype(bf16)


def spread(rank, fields, chunks):
    lane = lax.broadcasted_iota(jnp.int32, rank.shape, 1).astype(f32) + mark
    hot = [jnp.where(rank == lane + float(m * lanes), 1.0, 0.0).astype(bf16) for m in range(chunks)]
    return jnp.dot(fields, jnp.concatenate(hot, 1), preferred_element_type=f32)


def put_list(rows, start, low, high, number, spare):
    for m in range(low.shape[1] // lanes):
        lane = lax.broadcasted_iota(jnp.int32, (1, lanes), 1) + m * lanes
        part = slice(m * lanes, (m + 1) * lanes)
        value = (low[:, part] + 256.0 * high[:, part]).astype(jnp.int32)
        rows[start + m : start + m + 1, :] = jnp.where(lane < number, value, spare)


def own_kernel(sizes, codes_of, pairs, count, own, right, weighed, left, todo, stage, rows, sem):
    bx, by, bz, _ = sizes
    total = bx * by * bz
    entries = pairs.shape[1]
    code = lax.broadcasted_iota(jnp.int32, (total * code_total, entries), 0)
    hot = jnp.where(code == pairs[...], 1.0, 0.0).astype(bf16)
    fields = jnp.dot(codes_of[...], hot, preferred_element_type=f32)
    alive = lax.broadcasted_iota(jnp.int32, (1, entries), 1) < count[0]
    marks = [jnp.where(alive, fields[k : k + 1], 0.0) for k in range(2, 6)]
    tall = jnp.concatenate([jnp.broadcast_to(v, (lanes, entries)) for v in marks], 0).astype(bf16)
    ranks = lax.dot_general(
        ranked(entries), tall, (((1,), (1,)), ((), ())), preferred_element_type=f32
    )
    ends = fields.astype(bf16)
    rows[...] = jnp.zeros_like(rows)
    lane = lax.broadcasted_iota(jnp.int32, (1, lanes), 1)
    numbers = jnp.zeros((1, lanes), jnp.int32)
    for k in range(4):
        both = spread(ranks[:, k * lanes : (k + 1) * lanes], ends, 2)
        number = jnp.sum(marks[k], 1, keepdims=True).astype(jnp.int32)
        low, high = (both[1:2], both[0:1]) if k == 1 else (both[0:1], both[1:2])
        put_list(rows, 2 * k, low, high, number, total)
        numbers = jnp.where(lane == k, number, numbers)
    rows[8:9, :] = numbers
    copy = pltpu.make_async_copy(rows, todo, sem)
    copy.start()
    shape_blocks(sizes, [(0, lambda d: own[d])], stage, right, weighed, left)
    left[total] = left[0]
    copy.wait()


def list_inbound(ranks_of, ends_of, sources, flags, rows, spare):
    base = 0
    for _, part in sources:
        height = part(9).shape[0]
        flags[base : base + height, :] = part(9)
        base += height
    by_code = [jnp.broadcast_to(flags[:, c : c + 1], (base, lanes)) for c in range(1, code_total)]
    tall = jnp.concatenate(by_code, 0).astype(bf16)
    rank = jnp.dot(ranks_of[...], tall, preferred_element_type=f32)
    both = spread(rank, ends_of[...], 2)
    number = rank[rank.shape[0] - 1 :, :].astype(jnp.int32)
    rows[...] = jnp.zeros_like(rows)
    put_list(rows, 0, both[0:1], both[1:2], number, spare)
    rows[2:3, :] = number


def add_step(lookup, start, width, right, weighed, left, acc):
    results = []
    for k in range(width):
        entry = lookup(start + k)
        row, col = entry & 255, entry >> 8
        square = lax.dot_general(
            right[col], left[row], (((0,), (0,)), ((), ())), preferred_element_type=f32
        )
        root = lax.rsqrt(square)
        weight = root * root * root
        high = weight.astype(bf16)
        low = (weight - high.astype(f32)).astype(bf16)
        both = jnp.dot(weighed[col], jnp.concatenate([high, low], 0), preferred_element_type=f32)
        results.append((row, both[0:16] + both[16:32]))
    for row, value in results:
        at_row = pl.ds(pl.multiple_of(row * 16, 16), 16)
        acc[at_row, :] += value


def interact(lookup, start, end, *refs):
    number = end - start
    steps = (number + unroll - 1 - short_steps[-1]) // unroll
    done = start + steps * unroll

    def whole(at, carry):
        add_step(lookup, start + at * unroll, unroll, *refs)
        return carry

    lax.fori_loop(0, steps, whole, 0)
    left_over = end - done
    least = 0
    for width in short_steps:

        @pl.when((left_over > least) & (left_over <= width))
        def _():
            add_step(lookup, done, width, *refs)

        least = width


def near_list(todo):
    n = todo[8, 0]
    number = n + todo[8, 1]
    return joined(todo, 0, n, todo, 2), jnp.minimum(number, first_share), number


def near_kernel(todo, right, weighed, left, acc):
    acc[...] = jnp.zeros_like(acc)
    lookup, middle, _ = near_list(todo)
    interact(lookup, 0, middle, right, weighed, left, acc)


def listed(rows, start):
    return lambda at: rows[start + (at >> 7), at & 127]


def joined(rows, start, number, more, then_start):
    first, then = listed(rows, start), listed(more, then_start)
    return lambda at: jnp.where(at < number, first(at), then(jnp.maximum(at - number, 0)))


def side_sources(sizes, groups, here, beside):
    bx, by, bz, cells = sizes
    heights = group_heights(bx, by, bz)
    mom_rows = 8 * cells // lanes
    x_start = parts_sent * heights[0]
    starts = {0: 0, 1: x_start, 2: x_start + parts_sent * heights[1] + mom_rows, 4: 0, 3: parts_sent * heights[3] + mom_rows}
    return [(g, rows_of((here, beside)[g >= 5], starts[g % 5], heights[g])) for g in groups]


def mid_kernel(sizes, ranks_of, ends_of, x_all, p_x_all, mom_in, todo, right, weighed, left, *refs):
    bx, by, bz, _ = sizes
    right_1, weighed_1, found, mom_out, acc, stage, flags, rows, sem = refs[-9:]
    sources = side_sources(sizes, set_groups(1), x_all, p_x_all)
    list_inbound(ranks_of, ends_of, sources, flags, rows, bx * by * bz)
    copy = pltpu.make_async_copy(rows, found, sem)
    copy.start()
    mom_out[...] = mom_in[...]
    shape_blocks(sizes, sources, stage, right_1, weighed_1)
    acc[...] = jnp.zeros_like(acc)
    lookup, middle, number = near_list(todo)
    interact(lookup, middle, number, right, weighed, left, acc)
    copy.wait()


def side_kernel(todo, found, right, weighed, left, _, acc):
    acc[...] = jnp.zeros_like(acc)
    n = todo[8, 2]
    interact(joined(todo, 4, n, found, 0), 0, n + found[2, 0], right, weighed, left, acc)


def coarse_place(sizes, axes, chunk):
    bx, by, bz, _ = sizes
    coarse = (bx // 2, by // 2, bz // 2)
    number = lax.broadcasted_iota(jnp.int32, (1, lanes), 1) + chunk * lanes
    places = []
    for d in (2, 1, 0):
        places.append(number % coarse[d])
        number = number // coarse[d]
    for k, d in enumerate((2, 1, 0)):
        size = lax.axis_size(axes[d])
        places[k] = places[k] + number % size * coarse[d]
        number = number // size
    return places[::-1]


def close_kernel(sizes, axes, grid, moments, todo, ranks_of, ends_of, y_both, p_y_both, left, acc_a, acc_b, acc_c, own, *refs):
    bx, by, bz, cells = sizes
    total, face = bx * by * bz, by * bz
    mom_parts = refs[:-9]
    out, right, weighed, stage, acc, flags, rows, found, sem = refs[-9:]
    sources = side_sources(sizes, set_groups(2), y_both, p_y_both)
    list_inbound(ranks_of, ends_of, sources, flags, rows, total)
    copy = pltpu.make_async_copy(rows, found, sem)
    copy.start()
    shape_blocks(sizes, sources, stage, right, weighed)
    acc[...] = acc_a[...] + acc_b[...] + acc_c[...]
    copy.wait()
    n = todo[8, 3]
    interact(joined(todo, 6, n, found, 0), 0, n + found[2, 0], right, weighed, left, acc)
    mom = moments(y_both, p_y_both, mom_parts)

    cx, cy, cz = bx // 2, by // 2, bz // 2
    deep = lax.broadcasted_iota(jnp.int32, (face, lanes), 0)
    local = (None, deep // (2 * bz), deep % bz // 2)
    far = [[] for _ in range(6)]
    for x in range(cx):
        totals = [jnp.zeros((face, lanes), f32)] * 6
        for chunk in range(cells // lanes):
            lengths = []
            cell_of = coarse_place(sizes, axes, chunk)
            for d, axis in enumerate(axes):
                at = lax.axis_index(axis) * (cx, cy, cz)[d] + (x if d == 0 else local[d])
                delta = at - cell_of[d]
                half = grid[d] // 2
                delta = jnp.where(delta >= grid[d] - half, delta - grid[d], delta)
                delta = jnp.where(delta < -half, delta + grid[d], delta)
                lengths.append(2.0 * delta.astype(f32))
            radius = lengths[0] * lengths[0] + lengths[1] * lengths[1] + lengths[2] * lengths[2]
            root = lax.rsqrt(radius + core_square)
            weight = jnp.where(radius == 0.0, 0.0, root * root * root)
            m = [mom[chunk * 8 + f : chunk * 8 + f + 1] for f in range(8)]
            turned = turn_rows([weight * v for v in lengths], m)
            totals = [t + v for t, v in zip(totals, turned)]
        for f in range(6):
            far[f].append(jnp.sum(totals[f], 1, keepdims=True))

    place = position(0, total, bx, by, bz)
    p = [own[d] + place[d] for d in range(3)]
    b = [own[3 + d] for d in range(3)]
    l = [own[6 + d] for d in range(3)]
    moment = [acc[pl.ds(f, total, stride=16), :] for f in range(8)]
    crossed = [acc[pl.ds(8 + f, total, stride=16), :] for f in range(6)]
    turned = turn_rows(p, moment)
    s = []
    for f in range(6):
        column = jnp.concatenate([far[f][x // 2] for x in range(bx)], 0)
        s.append(turned[f] - crossed[f] + column)
    push = [
        s[0] * b[0] + s[3] * b[1] + s[4] * b[2],
        s[3] * b[0] + s[1] * b[1] + s[5] * b[2],
        s[4] * b[0] + s[5] * b[1] + s[2] * b[2],
    ]
    out[0] = kernel_scale * (push[1] * l[2] - push[2] * l[1])
    out[1] = kernel_scale * (push[2] * l[0] - push[0] * l[2])
    out[2] = kernel_scale * (push[0] * l[1] - push[1] * l[0])


def shifted(value, axis, step):
    size = lax.axis_size(axis)
    return lax.ppermute(value, axis, [(i, (i + step) % size) for i in range(size)])


def ring_sum(value, axis):
    total = value
    for step in range(1, lax.axis_size(axis)):
        total = total + shifted(value, axis, step)
    return total


def beside_z(value, layers):
    size = lax.axis_size("gz")
    if size == 2:
        return shifted(value, "gz", 1)
    head = value.shape
    split = value.reshape(-1, layers, lanes)
    above = shifted(split[:, :1], "gz", -1)
    below = shifted(split[:, layers - 1 :], "gz", 1)
    middle = split[:, 1 : layers - 1]
    return jnp.concatenate([above, middle, below], 1).reshape(head)


def body(offsets, burgers, line, block_fill, near_pairs, pair_count):
    _, bx, by, bz, slots = offsets.shape
    axes = ("gx", "gy", "gz")
    sizes = [lax.axis_size(axis) for axis in axes]
    heights = group_heights(bx, by, bz)
    own, face, rim = heights[0], heights[1], heights[3]
    set_size = [sum(heights[g] for g in set_groups(which)) for which in range(3)]
    coarse = (bx // 2, by // 2, bz // 2)
    grid = tuple(c * n for c, n in zip(coarse, sizes))
    per_device = coarse[0] * coarse[1] * coarse[2]
    cells = per_device * sizes[0] * sizes[1] * sizes[2]
    mom_rows = 8 * cells // lanes
    kinds = (bx, by, bz, cells)
    entries = near_pairs.shape[0]
    vmem = pl.BlockSpec(memory_space=pltpu.VMEM)
    smem = pl.BlockSpec(memory_space=pltpu.SMEM)
    hbm = pl.BlockSpec(memory_space=pltpu.HBM)
    anywhere = pl.BlockSpec(memory_space=pl.ANY)
    shape = jax.ShapeDtypeStruct
    flat = lambda v: v.reshape(3, own, slots)
    far = lambda v: pltpu.with_memory_space_constraint(v, pltpu.HBM)

    tables = [jnp.asarray(v.astype(bf16)) for v in work_tables(bx, by, bz)]
    assert max(entries, tables[1].shape[0], tables[3].shape[0]) + unroll <= 2 * lanes

    def call(kernel, out_shape, in_specs, out_specs, scratch, name, cost, limit=12):
        return pl.pallas_call(
            kernel,
            out_shape=out_shape,
            in_specs=in_specs,
            out_specs=out_specs,
            scratch_shapes=scratch,
            compiler_params=pltpu.CompilerParams(vmem_limit_bytes=limit * 2**20),
            cost_estimate=pl.CostEstimate(flops=cost, bytes_accessed=cost, transcendentals=0),
            name=name,
        )

    face_shape = shape((parts_sent * face + mom_rows, lanes), f32)
    rim_shape = shape((parts_sent * rim + mom_rows, lanes), f32)
    mom_shape = shape((mom_rows, lanes), f32)
    acc_shape = shape(((own + 1) * 16, lanes), f32)
    mine, face_lo, face_hi, mom, pairs, codes_of, *inbound = call(
        functools.partial(pack_kernel, kinds, axes),
        [
            shape((parts_sent, own, lanes), f32),
            face_shape,
            face_shape,
            mom_shape,
            shape((1, entries), jnp.int32),
            *[shape(v.shape, v.dtype) for v in tables],
        ],
        [smem] + [hbm] * 10,
        [vmem] * 10,
        [
            pltpu.VMEM((bx, bz, by), jnp.int32),
            pltpu.VMEM((3, own, lanes), f32),
            pltpu.VMEM((3, own, lanes), f32),
            pltpu.VMEM((3, own, lanes), f32),
            pltpu.VMEM((own, lanes), jnp.int32),
            pltpu.SemaphoreType.DMA((10,)),
        ],
        "pack",
        10**6,
    )(
        pair_count,
        far(jnp.transpose(block_fill, (0, 2, 1))),
        far(flat(offsets)),
        far(flat(burgers)),
        far(flat(line)),
        far(near_pairs.reshape(1, -1)),
        *[far(v) for v in tables],
    )

    x_far = [shifted(mom, "gx", step) for step in range(2, sizes[0] - 1)]
    x_lo = shifted(face_hi, "gx", 1)
    x_hi = shifted(face_lo, "gx", -1)
    right, weighed, left, todo = call(
        functools.partial(own_kernel, kinds),
        [
            shape((own, 32, lanes), bf16),
            shape((own, 32, 2 * lanes), bf16),
            shape((own + 1, 32, lanes), bf16),
            pltpu.SMEM((16, lanes), jnp.int32),
        ],
        [vmem, vmem, smem, vmem],
        [vmem, vmem, vmem, smem],
        [
            pltpu.VMEM((own * 80, lanes), f32),
            pltpu.VMEM((16, lanes), jnp.int32),
            pltpu.SemaphoreType.DMA,
        ],
        "own",
        10**7,
    )(codes_of, pairs, pair_count, mine)
    acc_a = call(
        near_kernel,
        acc_shape,
        [smem, vmem, vmem, vmem],
        vmem,
        [],
        "near",
        10**7,
    )(todo, right, weighed, left)
    side_lo, side_hi, x_all, mom_x = call(
        functools.partial(rim_kernel, kinds, sizes[0] > 2),
        [
            rim_shape,
            rim_shape,
            shape((parts_sent * (own + 2 * face) + 2 * mom_rows, lanes), f32),
            mom_shape,
        ],
        [vmem] * 4 + [anywhere] + [vmem] * len(x_far),
        [vmem] * 4,
        [],
        "rim",
        10**6,
    )(mine, mom, x_lo, x_hi, acc_a, *x_far)
    y_lo = shifted(side_hi, "gy", 1)
    y_hi = shifted(side_lo, "gy", -1)
    y_far = [shifted(mom_x, "gy", step) for step in range(2, sizes[1] - 1)]
    p_x_all = beside_z(x_all, bz)
    right_1, weighed_1, found, mom_kept, acc_b = call(
        functools.partial(mid_kernel, kinds),
        [
            shape((set_size[1], 32, lanes), bf16),
            shape((set_size[1], 32, 2 * lanes), bf16),
            pltpu.SMEM((8, lanes), jnp.int32),
            mom_shape,
            acc_shape,
        ],
        [vmem] * 5 + [smem, vmem, vmem, vmem, anywhere, anywhere],
        [vmem, vmem, smem, vmem, vmem],
        [
            pltpu.VMEM((set_size[1] * 80, lanes), f32),
            pltpu.VMEM((set_size[1], lanes), f32),
            pltpu.VMEM((8, lanes), jnp.int32),
            pltpu.SemaphoreType.DMA,
        ],
        "mid",
        10**7,
    )(*inbound[:2], x_all, p_x_all, mom_x, todo, right, weighed, left, side_lo, side_hi)
    for v in y_far:
        mom_kept = mom_kept + v
    y_both = jnp.concatenate([y_hi, y_lo, mom_kept], 0)
    p_y_both = beside_z(y_both, bz)

    acc_c = call(
        side_kernel,
        acc_shape,
        [smem, smem, vmem, vmem, vmem, anywhere],
        vmem,
        [],
        "side",
        10**7,
    )(todo, found, right_1, weighed_1, left, y_both)
    tail = parts_sent * rim
    if sizes[2] == 2:
        mom_parts = []

        def moments(y_both, p_y_both, parts):
            spans = [slice(tail, tail + mom_rows)]
            if sizes[1] > 2:
                spans.append(slice(2 * tail + mom_rows, 2 * (tail + mom_rows)))
            spans.append(slice(2 * (tail + mom_rows), 2 * tail + 3 * mom_rows))
            return sum(y_both[span] + p_y_both[span] for span in spans)

    else:
        mom_parts = [ring_sum(mom_kept + y_lo[tail:] + y_hi[tail:], "gz")]
        moments = lambda y_both, p_y_both, parts: parts[0][...]

    forces = call(
        functools.partial(close_kernel, kinds, axes, grid, moments),
        shape((3, own, lanes), f32),
        [smem] + [vmem] * (9 + len(mom_parts)),
        vmem,
        [
            pltpu.VMEM((set_size[2], 32, lanes), bf16),
            pltpu.VMEM((set_size[2], 32, 2 * lanes), bf16),
            pltpu.VMEM(((set_size[2] + 8) * 80, lanes), f32),
            pltpu.VMEM(((own + 1) * 16, lanes), f32),
            pltpu.VMEM((set_size[2], lanes), f32),
            pltpu.VMEM((8, lanes), jnp.int32),
            pltpu.SMEM((8, lanes), jnp.int32),
            pltpu.SemaphoreType.DMA,
        ],
        "close",
        10**7,
    )(todo, *inbound[2:], y_both, p_y_both, left, acc_a, acc_b, acc_c, mine, *mom_parts)
    return forces.reshape(3, bx, by, bz, slots)


def solution(mesh):
    in_specs = (
        P(None, "gx", "gy", "gz", None),
        P(None, "gx", "gy", "gz", None),
        P(None, "gx", "gy", "gz", None),
        P("gx", "gy", "gz"),
        P(("gx", "gy", "gz")),
        P(("gx", "gy", "gz")),
    )
    out_specs = P(None, "gx", "gy", "gz", None)
    return jax.shard_map(body, mesh=mesh, in_specs=in_specs, out_specs=out_specs, check_vma=False)
```

profile of v0, /device:TPU:0, one launch (start us, length us, event | category | flops | bytes accessed | tf_op | source)
XLA Modules:
  0.0 23.3 jit_solution(14367499190458040964)
XLA Ops:
  0.7 1.2 %pack.1 = (f32[10,32,128]{2,1,0:T(8,128)S(1)}, f32[88,128]{1,0:T(8,128)S(1)}, f32[88,128]{1,0:T(8,128)S(1)}, f32[8,128]{1,0:T(8,128)S(1)}, s32[1,192]{1,0:T(1,12...) custom-call(s32[1]{0:T(128)S(6)} %copy.12.count, ...), custom_call_target="tpu_custom_call" | custom-call | flops 1000000 | bytes 1000000 | tf_op jit(solution)/shard_map/pack/pallas_call | solution.py:620
  1.9 3.1 %collective-permute-start = (f32[88,128]{1,0:T(8,128)S(1)}, f32[88,128]{1,0:T(8,128)S(1)}, u32[]{:S(2)}, u32[]{:S(2)}) collective-permute-start(f32[88,128]{1,0:T(8,128)S(1)} %get-tuple-element.35), channel_id=1, source_target_pairs={{0,8},{8,16},{16,24},{24,0},{1,9},{9,17},{17,25},{25,1},{2,10},{10... | collective-permute-start | bytes 135176 | tf_op jit(solution)/shard_map/ppermute | solution.py:557
  5.0 2.1 %collective-permute-start.1 = (f32[88,128]{1,0:T(8,128)S(1)}, f32[88,128]{1,0:T(8,128)S(1)}, u32[]{:S(2)}, u32[]{:S(2)}) collective-permute-start(f32[88,128]{1,0:T(8,128)S(1)} %get-tuple-element.36), channel_id=1, source_target_pairs={{0,24},{8,0},{16,8},{24,16},{1,25},{9,1},{17,9},{25,17},{2,26},{10... | collective-permute-start | bytes 135176 | tf_op jit(solution)/shard_map/ppermute | solution.py:557
  7.1 0.9 %collective-permute-start.2 = (f32[8,128]{1,0:T(8,128)S(1)}, f32[8,128]{1,0:T(8,128)S(1)}, u32[]{:S(2)}, u32[]{:S(2)}) collective-permute-start(f32[8,128]{1,0:T(8,128)S(1)} %get-tuple-element.34.mom), channel_id=1, source_target_pairs={{0,16},{8,24},{16,0},{24,8},{1,17},{9,25},{17,1},{25,9},{2,18},{10... | collective-permute-start | bytes 12296 | tf_op jit(solution)/shard_map/ppermute | solution.py:557
  8.0 1.5 %own.1 = (bf16[32,32,128]{2,1,0:T(8,128)(2,1)S(1)}, bf16[32,32,256]{2,1,0:T(8,128)(2,1)S(1)}, bf16[33,32,128]{2,1,0:T(8,128)(2,1)S(1)}, s32[16,128]{1,0:T(8,128)S(4)}) custom-call(bf16[8,448]{1,0:T(8,128)(2,1)S(1)} %get-tuple-element.28.codes_of, s32[1,192]{1,0:T(1,128)S(1)} %get-tuple-element.29.pairs, s32[1]{0:T(128)S(6)} %copy.12.count, ...), custom_call_target="tpu_custom_call" | custom-call | flops 10000000 | bytes 10000000 | tf_op jit(solution)/shard_map/own/pallas_call | solution.py:655
  9.5 1.5 %near.1.refs_0_.acc_a = f32[528,128]{1,0:T(8,128)S(1)} custom-call(s32[16,128]{1,0:T(8,128)S(4)} %get-tuple-element.31.todo, bf16[32,32,128]{2,1,0:T(8,128)(2,1)S(1)} %get-tuple-element.37.right, bf16[32,32,256]{2,1,0:T(8,128)(2,1)S(1)} %get-tuple-element.38.weighed, bf16[33,32,128]{2,1,0:T(8,128)(2,1)S(1)} %get-tuple-element.39.left), custom_call_target="tpu_custom_call" | custom-call | flops 10000000 | bytes 10000000 | tf_op jit(solution)/shard_map/near/pallas_call | solution.py:673
  11.0 0.6 %collective-permute-done.2.refs_1_ = f32[8,128]{1,0:T(8,128)S(1)} collective-permute-done((f32[8,128]{1,0:T(8,128)S(1)}, f32[8,128]{1,0:T(8,128)S(1)}, u32[]{:S(2)}, u32[]{:S(2)}) %collective-permute-start.2) | collective-permute-done | bytes 4128 | tf_op jit(solution)/shard_map/ppermute | solution.py:557
  11.6 0.0 collective-permute-done.x_lo
  11.6 0.0 collective-permute-done.1.x_hi
  11.6 0.1 rim.1
  11.6 0.1 collective-permute-start.5
  11.7 1.7 %collective-permute-start.4 = (f32[128,128]{1,0:T(8,128)S(1)}, f32[128,128]{1,0:T(8,128)S(1)}, u32[]{:S(2)}, u32[]{:S(2)}) collective-permute-start(f32[128,128]{1,0:T(8,128)S(1)} %get-tuple-element.41.refs_1_), channel_id=1, source_target_pairs={{0,2},{2,4},{4,6},{6,0},{1,3},{3,5},{5,7},{7,1},{8,10},{10,12},{12... | collective-permute-start | bytes 196616 | tf_op jit(solution)/shard_map/ppermute | solution.py:557
  13.4 1.3 %collective-permute-start.3 = (f32[128,128]{1,0:T(8,128)S(1)}, f32[128,128]{1,0:T(8,128)S(1)}, u32[]{:S(2)}, u32[]{:S(2)}) collective-permute-start(f32[128,128]{1,0:T(8,128)S(1)} %get-tuple-element.40.refs_0_), channel_id=1, source_target_pairs={{0,6},{2,0},{4,2},{6,4},{1,7},{3,1},{5,3},{7,5},{8,14},{10,8},{12,... | collective-permute-start | bytes 196616 | tf_op jit(solution)/shard_map/ppermute | solution.py:557
  14.7 1.7 %collective-permute-start.6 = (f32[8,128]{1,0:T(8,128)S(1)}, f32[8,128]{1,0:T(8,128)S(1)}, u32[]{:S(2)}, u32[]{:S(2)}) collective-permute-start(f32[8,128]{1,0:T(8,128)S(1)} %get-tuple-element.45.mom_in), channel_id=1, source_target_pairs={{0,4},{2,6},{4,0},{6,2},{1,5},{3,7},{5,1},{7,3},{8,12},{10,14},{12... | collective-permute-start | bytes 12296 | tf_op jit(solution)/shard_map/ppermute | solution.py:557
  16.4 0.0 collective-permute-done.5.p_x_all
  16.4 1.4 %mid.1 = (bf16[64,32,128]{2,1,0:T(8,128)(2,1)S(1)}, bf16[64,32,256]{2,1,0:T(8,128)(2,1)S(1)}, s32[8,128]{1,0:T(8,128)S(4)}, f32[8,128]{1,0:T(8,128)S(1)}, f32[528,128]{1,0:T(8,128)S(1)}) custom-call(bf16[176,832]{1,0:T(8,128)(2,1)S(1)} %get-tuple-element.42.ranks_of, bf16[8,176]{1,0:T(8,128)(2,1)S(1)} %get-tuple-element.43.ends_of, ...), custom_call_target="tpu_custom_call" | custom-call | flops 10000000 | bytes 10000000 | tf_op jit(solution)/shard_map/mid/pallas_call | solution.py:700
  17.8 0.5 %collective-permute-done.6 = f32[8,128]{1,0:T(8,128)S(1)} collective-permute-done((f32[8,128]{1,0:T(8,128)S(1)}, f32[8,128]{1,0:T(8,128)S(1)}, u32[]{:S(2)}, u32[]{:S(2)}) %collective-permute-start.6) | collective-permute-done | bytes 4128 | tf_op jit(solution)/shard_map/ppermute | solution.py:557
  18.3 0.0 collective-permute-done.4
  18.3 0.4 %collective-permute-done.3 = f32[128,128]{1,0:T(8,128)S(1)} collective-permute-done((f32[128,128]{1,0:T(8,128)S(1)}, f32[128,128]{1,0:T(8,128)S(1)}, u32[]{:S(2)}, u32[]{:S(2)}) %collective-permute-start.3) | collective-permute-done | bytes 65568 | tf_op jit(solution)/shard_map/ppermute | solution.py:557
  18.7 0.1 collective-permute-start.7
  18.8 1.4 %side.1.acc_c = f32[528,128]{1,0:T(8,128)S(1)} custom-call(s32[16,128]{1,0:T(8,128)S(4)} %get-tuple-element.31.todo, s32[8,128]{1,0:T(8,128)S(4)} %get-tuple-element.48.found, bf16[64,32,128]{2,1,0:T(8,128)(2,1)S(1)} %get-tuple-element.49.right, bf16[64,32,256]{2,1,0:T(8,128)(2,1)S(1)} %get-tuple-element.50.weighed, ...), custom_call_target="tpu_custom_call" | custom-call | flops 10000000 | bytes 10000000 | tf_op jit(solution)/shard_map/side/pallas_call | solution.py:725
  20.2 0.0 collective-permute-done.7.p_y_both
  20.2 2.9 %close.1 = f32[3,32,128]{2,1,0:T(8,128)} custom-call(s32[16,128]{1,0:T(8,128)S(4)} %get-tuple-element.31.todo, bf16[80,624]{1,0:T(8,128)(2,1)S(1)} %get-tuple-element.32.ranks_of, bf16[8,80]{1,0:T(8,128)(2,1)S(1)} %get-tuple-element.33.ends_of, f32[264,128]{1,0:T(8,128)S(1)} %pad_maximum_fusion._.y_both, f32[264,128]{1,0:T(8,128)S(1)} %collective-permute-done.7.p_y_both, ...), custom_call_target="tpu_custom_call" | custom-call | flops 10000000 | bytes 10000000 | tf_op jit(solution)/shard_map/close/pallas_call | solution.py:749
  (2 shorter events, 0.0 us)
Async XLA Ops:
  1.9 9.7 %collective-permute-start = (f32[88,128]{1,0:T(8,128)S(1)}, f32[88,128]{1,0:T(8,128)S(1)}, u32[]{:S(2)}, u32[]{:S(2)}) collective-permute-start(f32[88,128]{1,0:T(8,128)S(1)} %get-tuple-element.35), channel_id=1, source_target_pairs={{0,8},{8,16},{16,24},{24,0},{1,9},{9,17},{17,25},{25,1},{2,10},{10... | collective-permute-start | bytes 135176 | tf_op jit(solution)/shard_map/ppermute | solution.py:557
  5.0 6.6 %collective-permute-start.1 = (f32[88,128]{1,0:T(8,128)S(1)}, f32[88,128]{1,0:T(8,128)S(1)}, u32[]{:S(2)}, u32[]{:S(2)}) collective-permute-start(f32[88,128]{1,0:T(8,128)S(1)} %get-tuple-element.36), channel_id=1, source_target_pairs={{0,24},{8,0},{16,8},{24,16},{1,25},{9,1},{17,9},{25,17},{2,26},{10... | collective-permute-start | bytes 135176 | tf_op jit(solution)/shard_map/ppermute | solution.py:557
  7.1 4.5 %collective-permute-start.2 = (f32[8,128]{1,0:T(8,128)S(1)}, f32[8,128]{1,0:T(8,128)S(1)}, u32[]{:S(2)}, u32[]{:S(2)}) collective-permute-start(f32[8,128]{1,0:T(8,128)S(1)} %get-tuple-element.34.mom), channel_id=1, source_target_pairs={{0,16},{8,24},{16,0},{24,8},{1,17},{9,25},{17,1},{25,9},{2,18},{10... | collective-permute-start | bytes 12296 | tf_op jit(solution)/shard_map/ppermute | solution.py:557
  11.6 4.7 %collective-permute-start.5 = (f32[496,128]{1,0:T(8,128)S(1)}, f32[496,128]{1,0:T(8,128)S(1)}, u32[]{:S(2)}, u32[]{:S(2)}) collective-permute-start(f32[496,128]{1,0:T(8,128)S(1)} %get-tuple-element.44.x_all), channel_id=1, source_target_pairs={{0,1},{1,0},{2,3},{3,2},{4,5},{5,4},{6,7},{7,6},{8,9},{9,8},{10,11... | collective-permute-start | bytes 761864 | tf_op jit(solution)/shard_map/ppermute | solution.py:557
  11.7 6.6 %collective-permute-start.4 = (f32[128,128]{1,0:T(8,128)S(1)}, f32[128,128]{1,0:T(8,128)S(1)}, u32[]{:S(2)}, u32[]{:S(2)}) collective-permute-start(f32[128,128]{1,0:T(8,128)S(1)} %get-tuple-element.41.refs_1_), channel_id=1, source_target_pairs={{0,2},{2,4},{4,6},{6,0},{1,3},{3,5},{5,7},{7,1},{8,10},{10,12},{12... | collective-permute-start | bytes 196616 | tf_op jit(solution)/shard_map/ppermute | solution.py:557
  13.4 5.3 %collective-permute-start.3 = (f32[128,128]{1,0:T(8,128)S(1)}, f32[128,128]{1,0:T(8,128)S(1)}, u32[]{:S(2)}, u32[]{:S(2)}) collective-permute-start(f32[128,128]{1,0:T(8,128)S(1)} %get-tuple-element.40.refs_0_), channel_id=1, source_target_pairs={{0,6},{2,0},{4,2},{6,4},{1,7},{3,1},{5,3},{7,5},{8,14},{10,8},{12,... | collective-permute-start | bytes 196616 | tf_op jit(solution)/shard_map/ppermute | solution.py:557
  14.7 3.6 %collective-permute-start.6 = (f32[8,128]{1,0:T(8,128)S(1)}, f32[8,128]{1,0:T(8,128)S(1)}, u32[]{:S(2)}, u32[]{:S(2)}) collective-permute-start(f32[8,128]{1,0:T(8,128)S(1)} %get-tuple-element.45.mom_in), channel_id=1, source_target_pairs={{0,4},{2,6},{4,0},{6,2},{1,5},{3,7},{5,1},{7,3},{8,12},{10,14},{12... | collective-permute-start | bytes 12296 | tf_op jit(solution)/shard_map/ppermute | solution.py:557
  18.7 1.5 %collective-permute-start.7 = (f32[264,128]{1,0:T(8,128)S(1)}, f32[264,128]{1,0:T(8,128)S(1)}, u32[]{:S(2)}, u32[]{:S(2)}) collective-permute-start(f32[264,128]{1,0:T(8,128)S(1)} %pad_maximum_fusion._.y_both), channel_id=1, source_target_pairs={{0,1},{1,0},{2,3},{3,2},{4,5},{5,4},{6,7},{7,6},{8,9},{9,8},{10,11... | collective-permute-start | bytes 405512 | tf_op jit(solution)/shard_map/ppermute | solution.py:557
where the time goes:
time: 23.7 us; the launch traced here: 23.3 us
  starting transfers between devices  10.9 us (46%)
  Pallas kernels  9.96 us (42%)
  waiting for transfers between devices  1.51 us (6%)
  between operations  0.89 us (4%)
    ppermute x8, starting transfers between devices, shifted(): lax.ppermute(value, axis, [(i, (i + step) % size) for i in range(size)])  10.9 us
    pallas_call x1, Pallas kernels, body(): call(functools.partial(close_kernel, kinds, axes, grid, moments), shape((...  2.92 us
    ppermute x8, waiting for transfers between devices, shifted(): lax.ppermute(value, axis, [(i, (i + step) % size) for i in range(size)])  1.51 us
    pallas_call x1, Pallas kernels, body(): call(functools.partial(own_kernel, kinds), [shape((own, 32, lanes), bf16)...  1.51 us
    pallas_call x1, Pallas kernels, body(): call(near_kernel, acc_shape, [smem, vmem, vmem, vmem], vmem, [], 'near',...  1.46 us
    pallas_call x1, Pallas kernels, body(): call(functools.partial(mid_kernel, kinds), [shape((set_size[1], 32, lanes...  1.41 us
    pallas_call x1, Pallas kernels, body(): call(side_kernel, acc_shape, [smem, smem, vmem, vmem, vmem, anywhere], vm...  1.36 us
    pallas_call x1, Pallas kernels, body(): call(functools.partial(pack_kernel, kinds, axes), [shape((parts_sent, own...  1.23 us
  transfers between devices with their start and end apart: 8, of which 3 were waited for; matrix products, arithmetic and copies ran while one was open for 0% of the time, Pallas kernels for 25%

commit v1 on v0

--- a/solution.py
+++ b/solution.py
@@ -242,38 +242,51 @@
         copy.wait()
 
 
-def rim_kernel(sizes, both_ways, own, mom, x_lo, x_hi, *refs):
+def rim_kernel(sizes, axes, both_ways, own, mom, x_lo_in, x_hi_in, *refs):
     bx, by, bz, _ = sizes
     face = by * bz
-    (face_lo, face_hi, x_all, mom_x), more = refs[-4:], refs[1:-4]
-    for y, out in ((0, face_lo), (by - 1, face_hi)):
-        for d in range(parts_sent):
-            to, at = d * (bx + 2) * bz, y * bz
-            for x in range(bx + 2):
-                if x == 0 or x == bx + 1:
-                    start = d * face + at
-                    rows = (x_lo if x == 0 else x_hi)[start : start + bz]
-                else:
-                    start = (x - 1) * face + at
-                    rows = own[d, start : start + bz]
-                out[to + x * bz : to + (x + 1) * bz] = rows
+    (side_1, side_2, x_all, mom_x), more = refs[-4:], refs[1:-4]
+    odd_y = lax.rem(lax.axis_index(axes[1]), 2) == 1
     total = bx * by * bz
     for d in range(parts_sent):
         x_all[d * total : (d + 1) * total] = own[d]
-    start = parts_sent * total
-    for v in (x_lo, x_hi):
-        x_all[start : start + v.shape[0]] = v[...]
-        start += v.shape[0]
+    start, tall = parts_sent * total, x_lo_in.shape[0]
+    x_lo, x_hi = x_lo_in[...], x_hi_in[...]
+    x_all[start : start + tall] = x_lo
+    x_all[start + tall : start + 2 * tall] = x_hi
+
+    def side(d, y):
+        rows = [x_lo[d * face + y * bz : d * face + (y + 1) * bz]]
+        for x in range(bx):
+            rows.append(own[d, x * face + y * bz : x * face + (y + 1) * bz])
+        return rows + [x_hi[d * face + y * bz : d * face + (y + 1) * bz]]
+
+    for d in range(parts_sent):
+        for x, (lo, hi) in enumerate(zip(side(d, 0), side(d, by - 1))):
+            at = (d * (bx + 2) + x) * bz
+            side_1[at : at + bz] = jnp.where(odd_y, lo, hi)
+            side_2[at : at + bz] = jnp.where(odd_y, hi, lo)
     head = parts_sent * face
-    total = mom[...] + x_lo[head:]
+    sums = mom[...] + x_lo[head:]
     if both_ways:
-        total = total + x_hi[head:]
+        sums = sums + x_hi[head:]
     for v in more:
-        total = total + v[...]
-    mom_x[...] = total
+        sums = sums + v[...]
+    mom_x[...] = sums
     head = parts_sent * (bx + 2) * bz
-    face_lo[head:] = total
-    face_hi[head:] = total
+    side_1[head:] = sums
+    side_2[head:] = sums
+
+
+def join_kernel(axes, y_2, y_1, *refs):
+    odd = lax.rem(lax.axis_index(axes[1]), 2) == 1
+    out, tall = refs[-1], y_1.shape[0]
+    out[0:tall] = jnp.where(odd, y_1[...], y_2[...])
+    out[tall : 2 * tall] = jnp.where(odd, y_2[...], y_1[...])
+    sums = refs[0][...]
+    for v in refs[1:-1]:
+        sums = sums + v[...]
+    out[2 * tall :] = sums
 
 
 def shape_blocks(sizes, sources, stage, right, weighed, left=None):
@@ -450,7 +463,7 @@
     heights = group_heights(bx, by, bz)
     mom_rows = 8 * cells // lanes
     x_start = parts_sent * heights[0]
-    starts = {0: 0, 1: x_start, 2: x_start + parts_sent * heights[1] + mom_rows, 4: 0, 3: parts_sent * heights[3] + mom_rows}
+    starts = {0: 0, 1: x_start, 2: x_start + parts_sent * heights[1] + mom_rows, 3: 0, 4: parts_sent * heights[3] + mom_rows}
     return [(g, rows_of((here, beside)[g >= 5], starts[g % 5], heights[g])) for g in groups]
 
 
@@ -555,6 +568,13 @@
 def shifted(value, axis, step):
     size = lax.axis_size(axis)
     return lax.ppermute(value, axis, [(i, (i + step) % size) for i in range(size)])
+
+
+def exchanged(value, axis, turn):
+    size = lax.axis_size(axis)
+    return lax.ppermute(
+        value, axis, [(i, (i + (1 if (i + turn) % 2 == 0 else -1)) % size) for i in range(size)]
+    )
 
 
 def ring_sum(value, axis):
@@ -679,8 +699,8 @@
         "near",
         10**7,
     )(todo, right, weighed, left)
-    side_lo, side_hi, x_all, mom_x = call(
-        functools.partial(rim_kernel, kinds, sizes[0] > 2),
+    side_1, side_2, x_all, mom_x = call(
+        functools.partial(rim_kernel, kinds, axes, sizes[0] > 2),
         [
             rim_shape,
             rim_shape,
@@ -693,8 +713,8 @@
         "rim",
         10**6,
     )(mine, mom, x_lo, x_hi, acc_a, *x_far)
-    y_lo = shifted(side_hi, "gy", 1)
-    y_hi = shifted(side_lo, "gy", -1)
+    y_1 = exchanged(side_1, "gy", 0)
+    y_2 = exchanged(side_2, "gy", 1)
     y_far = [shifted(mom_x, "gy", step) for step in range(2, sizes[1] - 1)]
     p_x_all = beside_z(x_all, bz)
     right_1, weighed_1, found, mom_kept, acc_b = call(
@@ -716,10 +736,16 @@
         ],
         "mid",
         10**7,
-    )(*inbound[:2], x_all, p_x_all, mom_x, todo, right, weighed, left, side_lo, side_hi)
-    for v in y_far:
-        mom_kept = mom_kept + v
-    y_both = jnp.concatenate([y_hi, y_lo, mom_kept], 0)
+    )(*inbound[:2], x_all, p_x_all, mom_x, todo, right, weighed, left, side_1, side_2)
+    y_both = call(
+        functools.partial(join_kernel, axes),
+        shape((2 * parts_sent * rim + 3 * mom_rows, lanes), f32),
+        [vmem] * (3 + len(y_far)),
+        vmem,
+        [],
+        "join",
+        10**5,
+    )(y_2, y_1, mom_kept, *y_far)
     p_y_both = beside_z(y_both, bz)
 
     acc_c = call(
@@ -743,7 +769,7 @@
             return sum(y_both[span] + p_y_both[span] for span in spans)
 
     else:
-        mom_parts = [ring_sum(mom_kept + y_lo[tail:] + y_hi[tail:], "gz")]
+        mom_parts = [ring_sum(y_both[tail : tail + mom_rows] + y_both[-2 * mom_rows - tail : -mom_rows - tail] if False else sum(y_both[k] for k in (slice(tail, tail + mom_rows), slice(2 * tail + mom_rows, 2 * tail + 2 * mom_rows), slice(2 * tail + 2 * mom_rows, None))), "gz")]
         moments = lambda y_both, p_y_both, parts: parts[0][...]
 
     forces = call(

time: 23.7 us -> 23.9 us (level)
  the two profiles are of different devices: /device:TPU:0 before, /device:TPU:1 now
where the time goes in v1:
time: 23.9 us; the launch traced here: 23.6 us
  Pallas kernels  11.1 us (46%)
  starting transfers between devices  9.63 us (40%)
  waiting for transfers between devices  1.98 us (8%)
  between operations  0.9 us (4%)
    ppermute x6, starting transfers between devices, shifted(): lax.ppermute(value, axis, [(i, (i + step) % size) for i in range(size)])  7.04 us
    pallas_call x1, Pallas kernels, body(): call(functools.partial(close_kernel, kinds, axes, grid, moments), shape((...  2.92 us
    ppermute x2, starting transfers between devices, exchanged(): lax.ppermute(value, axis, [(i, (i + (1 if (i + turn) % 2 == 0 else -1)) %...  2.59 us
    pallas_call x1, Pallas kernels, body(): call(near_kernel, acc_shape, [smem, vmem, vmem, vmem], vmem, [], 'near',...  2.31 us
    pallas_call x1, Pallas kernels, body(): call(side_kernel, acc_shape, [smem, smem, vmem, vmem, vmem, anywhere], vm...  1.63 us
    pallas_call x1, Pallas kernels, body(): call(functools.partial(own_kernel, kinds), [shape((own, 32, lanes), bf16)...  1.51 us
    pallas_call x1, Pallas kernels, body(): call(functools.partial(mid_kernel, kinds), [shape((set_size[1], 32, lanes...  1.42 us
    pallas_call x1, Pallas kernels, body(): call(functools.partial(pack_kernel, kinds, axes), [shape((parts_sent, own...  1.23 us
  transfers between devices with their start and end apart: 8, of which 2 were waited for; matrix products, arithmetic and copies ran while one was open for 0% of the time, Pallas kernels for 29%

profile of v1, /device:TPU:1, one launch (start us, length us, event | category | flops | bytes accessed | tf_op | source)
XLA Modules:
  0.0 23.6 jit_solution(17960025345736190661)
XLA Ops:
  0.7 1.2 %pack.1 = (f32[10,32,128]{2,1,0:T(8,128)S(1)}, f32[88,128]{1,0:T(8,128)S(1)}, f32[88,128]{1,0:T(8,128)S(1)}, f32[8,128]{1,0:T(8,128)S(1)}, s32[1,192]{1,0:T(1,12...) custom-call(s32[1]{0:T(128)S(6)} %copy.12.count, ...), custom_call_target="tpu_custom_call" | custom-call | flops 1000000 | bytes 1000000 | tf_op jit(solution)/shard_map/pack/pallas_call | solution.py:640
  1.9 2.2 %collective-permute-start = (f32[88,128]{1,0:T(8,128)S(1)}, f32[88,128]{1,0:T(8,128)S(1)}, u32[]{:S(2)}, u32[]{:S(2)}) collective-permute-start(f32[88,128]{1,0:T(8,128)S(1)} %get-tuple-element.35), channel_id=1, source_target_pairs={{0,8},{8,16},{16,24},{24,0},{1,9},{9,17},{17,25},{25,1},{2,10},{10... | collective-permute-start | bytes 135176 | tf_op jit(solution)/shard_map/ppermute | solution.py:570
  4.1 2.1 %collective-permute-start.1 = (f32[88,128]{1,0:T(8,128)S(1)}, f32[88,128]{1,0:T(8,128)S(1)}, u32[]{:S(2)}, u32[]{:S(2)}) collective-permute-start(f32[88,128]{1,0:T(8,128)S(1)} %get-tuple-element.36), channel_id=1, source_target_pairs={{0,24},{8,0},{16,8},{24,16},{1,25},{9,1},{17,9},{25,17},{2,26},{10... | collective-permute-start | bytes 135176 | tf_op jit(solution)/shard_map/ppermute | solution.py:570
  6.2 0.4 %collective-permute-start.2 = (f32[8,128]{1,0:T(8,128)S(1)}, f32[8,128]{1,0:T(8,128)S(1)}, u32[]{:S(2)}, u32[]{:S(2)}) collective-permute-start(f32[8,128]{1,0:T(8,128)S(1)} %get-tuple-element.34.mom), channel_id=1, source_target_pairs={{0,16},{8,24},{16,0},{24,8},{1,17},{9,25},{17,1},{25,9},{2,18},{10... | collective-permute-start | bytes 12296 | tf_op jit(solution)/shard_map/ppermute | solution.py:570
  6.6 1.5 %own.1 = (bf16[32,32,128]{2,1,0:T(8,128)(2,1)S(1)}, bf16[32,32,256]{2,1,0:T(8,128)(2,1)S(1)}, bf16[33,32,128]{2,1,0:T(8,128)(2,1)S(1)}, s32[16,128]{1,0:T(8,128)S(4)}) custom-call(bf16[8,448]{1,0:T(8,128)(2,1)S(1)} %get-tuple-element.28.codes_of, s32[1,192]{1,0:T(1,128)S(1)} %get-tuple-element.29.pairs, s32[1]{0:T(128)S(6)} %copy.12.count, ...), custom_call_target="tpu_custom_call" | custom-call | flops 10000000 | bytes 10000000 | tf_op jit(solution)/shard_map/own/pallas_call | solution.py:675
  8.1 2.3 %near.1.refs_0_.acc_a = f32[528,128]{1,0:T(8,128)S(1)} custom-call(s32[16,128]{1,0:T(8,128)S(4)} %get-tuple-element.31.todo, bf16[32,32,128]{2,1,0:T(8,128)(2,1)S(1)} %get-tuple-element.37.right, bf16[32,32,256]{2,1,0:T(8,128)(2,1)S(1)} %get-tuple-element.38.weighed, bf16[33,32,128]{2,1,0:T(8,128)(2,1)S(1)} %get-tuple-element.39.left), custom_call_target="tpu_custom_call" | custom-call | flops 10000000 | bytes 10000000 | tf_op jit(solution)/shard_map/near/pallas_call | solution.py:693
  10.4 0.0 collective-permute-done.2.refs_1_
  10.4 0.0 collective-permute-done.x_lo_in
  10.4 0.0 collective-permute-done.1.x_hi_in
  10.4 0.1 rim.1
  10.5 1.3 %collective-permute-start.5 = (f32[496,128]{1,0:T(8,128)S(1)}, f32[496,128]{1,0:T(8,128)S(1)}, u32[]{:S(2)}, u32[]{:S(2)}) collective-permute-start(f32[496,128]{1,0:T(8,128)S(1)} %get-tuple-element.44.x_all), channel_id=1, source_target_pairs={{0,1},{1,0},{2,3},{3,2},{4,5},{5,4},{6,7},{7,6},{8,9},{9,8},{10,11... | collective-permute-start | bytes 761864 | tf_op jit(solution)/shard_map/ppermute | solution.py:570
  11.8 2.3 %collective-permute-start.3 = (f32[128,128]{1,0:T(8,128)S(1)}, f32[128,128]{1,0:T(8,128)S(1)}, u32[]{:S(2)}, u32[]{:S(2)}) collective-permute-start(f32[128,128]{1,0:T(8,128)S(1)} %get-tuple-element.40.refs_1_), channel_id=1, source_target_pairs={{0,6},{2,4},{4,2},{6,0},{1,7},{3,5},{5,3},{7,1},{8,14},{10,12},{12... | collective-permute-start | bytes 196616 | tf_op jit(solution)/shard_map/ppermute | solution.py:575
  14.1 0.3 %collective-permute-start.4 = (f32[128,128]{1,0:T(8,128)S(1)}, f32[128,128]{1,0:T(8,128)S(1)}, u32[]{:S(2)}, u32[]{:S(2)}) collective-permute-start(f32[128,128]{1,0:T(8,128)S(1)} %get-tuple-element.41.refs_0_), channel_id=1, source_target_pairs={{0,2},{2,0},{4,6},{6,4},{1,3},{3,1},{5,7},{7,5},{8,10},{10,8},{12,... | collective-permute-start | bytes 196616 | tf_op jit(solution)/shard_map/ppermute | solution.py:575
  14.4 0.1 collective-permute-start.6
  14.4 0.0 collective-permute-done.5.p_x_all
  14.4 1.4 %mid.1 = (bf16[64,32,128]{2,1,0:T(8,128)(2,1)S(1)}, bf16[64,32,256]{2,1,0:T(8,128)(2,1)S(1)}, s32[8,128]{1,0:T(8,128)S(4)}, f32[8,128]{1,0:T(8,128)S(1)}, f32[528,128]{1,0:T(8,128)S(1)}) custom-call(bf16[176,832]{1,0:T(8,128)(2,1)S(1)} %get-tuple-element.42.ranks_of, bf16[8,176]{1,0:T(8,128)(2,1)S(1)} %get-tuple-element.43.ends_of, ...), custom_call_target="tpu_custom_call" | custom-call | flops 10000000 | bytes 10000000 | tf_op jit(solution)/shard_map/mid/pallas_call | solution.py:720
  15.9 1.0 %collective-permute-done.6.refs_1_ = f32[8,128]{1,0:T(8,128)S(1)} collective-permute-done((f32[8,128]{1,0:T(8,128)S(1)}, f32[8,128]{1,0:T(8,128)S(1)}, u32[]{:S(2)}, u32[]{:S(2)}) %collective-permute-start.6) | collective-permute-done | bytes 4128 | tf_op jit(solution)/shard_map/ppermute | solution.py:570
  16.8 0.0 collective-permute-done.3.y_2
  16.8 1.0 %collective-permute-done.4.y_1 = f32[128,128]{1,0:T(8,128)S(1)} collective-permute-done((f32[128,128]{1,0:T(8,128)S(1)}, f32[128,128]{1,0:T(8,128)S(1)}, u32[]{:S(2)}, u32[]{:S(2)}) %collective-permute-start.4) | collective-permute-done | bytes 65568 | tf_op jit(solution)/shard_map/ppermute | solution.py:575
  17.8 1.0 %collective-permute-start.7 = (f32[264,128]{1,0:T(8,128)S(1)}, f32[264,128]{1,0:T(8,128)S(1)}, u32[]{:S(2)}, u32[]{:S(2)}) collective-permute-start(f32[264,128]{1,0:T(8,128)S(1)} %join.1._.y_both), channel_id=1, source_target_pairs={{0,1},{1,0},{2,3},{3,2},{4,5},{5,4},{6,7},{7,6},{8,9},{9,8},{10,11... | collective-permute-start | bytes 405512 | tf_op jit(solution)/shard_map/ppermute | solution.py:570
  18.9 1.6 %side.1.acc_c = f32[528,128]{1,0:T(8,128)S(1)} custom-call(s32[16,128]{1,0:T(8,128)S(4)} %get-tuple-element.31.todo, s32[8,128]{1,0:T(8,128)S(4)} %get-tuple-element.48.found, bf16[64,32,128]{2,1,0:T(8,128)(2,1)S(1)} %get-tuple-element.49.right, bf16[64,32,256]{2,1,0:T(8,128)(2,1)S(1)} %get-tuple-element.50.weighed, ...), custom_call_target="tpu_custom_call" | custom-call | flops 10000000 | bytes 10000000 | tf_op jit(solution)/shard_map/side/pallas_call | solution.py:751
  20.5 0.0 collective-permute-done.7.p_y_both
  20.5 2.9 %close.1 = f32[3,32,128]{2,1,0:T(8,128)} custom-call(s32[16,128]{1,0:T(8,128)S(4)} %get-tuple-element.31.todo, bf16[80,624]{1,0:T(8,128)(2,1)S(1)} %get-tuple-element.32.ranks_of, bf16[8,80]{1,0:T(8,128)(2,1)S(1)} %get-tuple-element.33.ends_of, f32[264,128]{1,0:T(8,128)S(1)} %join.1._.y_both, f32[264,128]{1,0:T(8,128)S(1)} %collective-permute-done.7.p_y_both, ...), custom_call_target="tpu_custom_call" | custom-call | flops 10000000 | bytes 10000000 | tf_op jit(solution)/shard_map/close/pallas_call | solution.py:775
  (1 shorter events, 0.0 us)
Async XLA Ops:
  1.9 8.5 %collective-permute-start = (f32[88,128]{1,0:T(8,128)S(1)}, f32[88,128]{1,0:T(8,128)S(1)}, u32[]{:S(2)}, u32[]{:S(2)}) collective-permute-start(f32[88,128]{1,0:T(8,128)S(1)} %get-tuple-element.35), channel_id=1, source_target_pairs={{0,8},{8,16},{16,24},{24,0},{1,9},{9,17},{17,25},{25,1},{2,10},{10... | collective-permute-start | bytes 135176 | tf_op jit(solution)/shard_map/ppermute | solution.py:570
  4.1 6.3 %collective-permute-start.1 = (f32[88,128]{1,0:T(8,128)S(1)}, f32[88,128]{1,0:T(8,128)S(1)}, u32[]{:S(2)}, u32[]{:S(2)}) collective-permute-start(f32[88,128]{1,0:T(8,128)S(1)} %get-tuple-element.36), channel_id=1, source_target_pairs={{0,24},{8,0},{16,8},{24,16},{1,25},{9,1},{17,9},{25,17},{2,26},{10... | collective-permute-start | bytes 135176 | tf_op jit(solution)/shard_map/ppermute | solution.py:570
  6.2 4.2 %collective-permute-start.2 = (f32[8,128]{1,0:T(8,128)S(1)}, f32[8,128]{1,0:T(8,128)S(1)}, u32[]{:S(2)}, u32[]{:S(2)}) collective-permute-start(f32[8,128]{1,0:T(8,128)S(1)} %get-tuple-element.34.mom), channel_id=1, source_target_pairs={{0,16},{8,24},{16,0},{24,8},{1,17},{9,25},{17,1},{25,9},{2,18},{10... | collective-permute-start | bytes 12296 | tf_op jit(solution)/shard_map/ppermute | solution.py:570
  10.5 3.9 %collective-permute-start.5 = (f32[496,128]{1,0:T(8,128)S(1)}, f32[496,128]{1,0:T(8,128)S(1)}, u32[]{:S(2)}, u32[]{:S(2)}) collective-permute-start(f32[496,128]{1,0:T(8,128)S(1)} %get-tuple-element.44.x_all), channel_id=1, source_target_pairs={{0,1},{1,0},{2,3},{3,2},{4,5},{5,4},{6,7},{7,6},{8,9},{9,8},{10,11... | collective-permute-start | bytes 761864 | tf_op jit(solution)/shard_map/ppermute | solution.py:570
  11.8 5.1 %collective-permute-start.3 = (f32[128,128]{1,0:T(8,128)S(1)}, f32[128,128]{1,0:T(8,128)S(1)}, u32[]{:S(2)}, u32[]{:S(2)}) collective-permute-start(f32[128,128]{1,0:T(8,128)S(1)} %get-tuple-element.40.refs_1_), channel_id=1, source_target_pairs={{0,6},{2,4},{4,2},{6,0},{1,7},{3,5},{5,3},{7,1},{8,14},{10,12},{12... | collective-permute-start | bytes 196616 | tf_op jit(solution)/shard_map/ppermute | solution.py:575
  14.1 3.7 %collective-permute-start.4 = (f32[128,128]{1,0:T(8,128)S(1)}, f32[128,128]{1,0:T(8,128)S(1)}, u32[]{:S(2)}, u32[]{:S(2)}) collective-permute-start(f32[128,128]{1,0:T(8,128)S(1)} %get-tuple-element.41.refs_0_), channel_id=1, source_target_pairs={{0,2},{2,0},{4,6},{6,4},{1,3},{3,1},{5,7},{7,5},{8,10},{10,8},{12,... | collective-permute-start | bytes 196616 | tf_op jit(solution)/shard_map/ppermute | solution.py:575
  14.4 2.5 %collective-permute-start.6 = (f32[8,128]{1,0:T(8,128)S(1)}, f32[8,128]{1,0:T(8,128)S(1)}, u32[]{:S(2)}, u32[]{:S(2)}) collective-permute-start(f32[8,128]{1,0:T(8,128)S(1)} %get-tuple-element.45.mom_in), channel_id=1, source_target_pairs={{0,4},{2,6},{4,0},{6,2},{1,5},{3,7},{5,1},{7,3},{8,12},{10,14},{12... | collective-permute-start | bytes 12296 | tf_op jit(solution)/shard_map/ppermute | solution.py:570
  17.8 2.7 %collective-permute-start.7 = (f32[264,128]{1,0:T(8,128)S(1)}, f32[264,128]{1,0:T(8,128)S(1)}, u32[]{:S(2)}, u32[]{:S(2)}) collective-permute-start(f32[264,128]{1,0:T(8,128)S(1)} %join.1._.y_both), channel_id=1, source_target_pairs={{0,1},{1,0},{2,3},{3,2},{4,5},{5,4},{6,7},{7,6},{8,9},{9,8},{10,11... | collective-permute-start | bytes 405512 | tf_op jit(solution)/shard_map/ppermute | solution.py:570
